TPU v7x, 256 devices: a whole 4x4x8 slice. The times are simulated.
256 devices in a mesh: section: 8 (over y, z_hi), expert: 32 (over x, z_lo, core).
Axes of the slice: x: 4, y: 4, z: 8 (z_hi: 2, z_lo: 4; z = z_hi * 4 + z_lo), core: 2. Of those that a mesh axis runs over, the one named last changes fastest.
Arguments:
- act_fwd: bfloat16 [8, 4096, 4096], P('section', 'expert'), may hold values from -6 to 6
- act_rev: bfloat16 [8, 4096, 4096], P('section', 'expert'), may hold values from -6 to 6
- ids_fwd: int32 [8, 4096, 2], P('section', 'expert'), may hold values from 0 to 15, all different within a row; in each aligned block of 128 rows (0 to 127, 128 to 255, ..., all dimensions but the last counted through in order) at most 24 rows name the same one
- ids_rev: int32 [8, 4096, 2], P('section', 'expert'), may hold values from 0 to 15, all different within a row; in each aligned block of 128 rows (0 to 127, 128 to 255, ..., all dimensions but the last counted through in order) at most 24 rows name the same one
- probs_fwd: float32 [8, 4096, 2], P('section', 'expert'), may hold values from 0.05 to 1
- probs_rev: float32 [8, 4096, 2], P('section', 'expert'), may hold values from 0.05 to 1
- w_gate: bfloat16 [8, 4096, 12288], P('section', None, 'expert'), may hold values from -0.09375 to 0.09375
- w_up: bfloat16 [8, 4096, 12288], P('section', None, 'expert'), may hold values from -0.09375 to 0.09375
- w_down: bfloat16 [8, 12288, 4096], P('section', 'expert'), may hold values from -0.21875 to 0.21875
Outputs:
- out_fwd: bfloat16 [8, 4096, 4096], P('section', 'expert')
- out_rev: bfloat16 [8, 4096, 4096], P('section', 'expert')
Inputs may be any that keep to these rules, and one draw needn't show every extreme that they name: `ids_fwd`: each row names 2 different experts. Within the 128 rows of one device (aligned blocks) no expert is named by more than 24 rows, and some block reaches 24. `ids_rev`: as for ids_fwd.
All inputs are finite; a program needn't handle non-finite values.
Results may differ from a plain program's by a relative error of at most 0.0048.
Values may be sent and summed in bfloat16 or wider, within the bound.
No kernel may reach another device: no remote copies, remote signals or barrier semaphores. Data moves between devices by JAX's collectives and lax.ppermute only.
A program may use at most 128 MiB of HBM per device.

v0:
```python
import jax
import jax.numpy as jnp
from jax import lax
from jax.sharding import Mesh
from jax.sharding import PartitionSpec as P

EXPERTS = 16
CAP = 24
X, Z, Y = (4, 4, 4)
BF = jnp.bfloat16
F32 = jnp.float32


def slots_of(ids):
    flat = ids.reshape(-1)
    n = flat.shape[0]
    one_hot = (flat[:, None] == jnp.arange(EXPERTS, dtype=jnp.int32)[None, :]).astype(BF)
    place = jnp.arange(n, dtype=jnp.int32)
    below = (place[:, None] > place[None, :]).astype(BF)
    counts = jnp.dot(below, one_hot, preferred_element_type=F32)
    rank = jnp.sum(counts * one_hot.astype(F32), axis=1).astype(jnp.int32)
    return (flat * CAP + rank).reshape(ids.shape)


def outgoing(tokens, slots, z_lo):
    t = slots.shape[1]
    row = jnp.arange(X * Z * CAP, dtype=jnp.int32)
    to_x, source, rank = (row // (Z * CAP), row // CAP % Z, row % CAP)
    target = (to_x * Z + z_lo) * CAP + rank
    held = jnp.arange(Z * t, dtype=jnp.int32) // t
    flat = slots.reshape(Z * t, 2)
    hit = (flat[None, :, 0] == target[:, None]) | (flat[None, :, 1] == target[:, None])
    pick = (hit & (held[None, :] == source[:, None])).astype(BF)
    return jnp.dot(pick, tokens, preferred_element_type=F32).astype(BF)


def expert(rows, w_gate, w_up, w_down):
    gate = jnp.dot(rows, w_gate, preferred_element_type=F32)
    up = jnp.dot(rows, w_up, preferred_element_type=F32)
    hidden = (jax.nn.silu(gate) * up).astype(BF)
    return jnp.dot(hidden, w_down, preferred_element_type=F32).astype(BF)


def combine(home, back, slots, probs):
    gates = probs / jnp.sum(probs, axis=1, keepdims=True)
    place = jnp.arange(EXPERTS * CAP, dtype=jnp.int32)
    mix = jnp.sum(
        jnp.where(slots[:, :, None] == place[None, None, :], gates[:, :, None], 0.0), axis=1
    )
    high = lax.reduce_precision(mix, 8, 7)
    both = jnp.concatenate([high, mix - high], axis=0).astype(BF)
    summed = jnp.dot(both, back, preferred_element_type=F32)
    t = home.shape[0]
    return (home.astype(F32) + (summed[:t] + summed[t:])).astype(BF)


def after(value, *others):
    return lax.optimization_barrier((value, *others))[0]


def body(act_fwd, act_rev, ids_fwd, ids_rev, probs_fwd, probs_rev, w_gate, w_up, w_down):
    z_hi, z_lo = (lax.axis_index("z_hi"), lax.axis_index("z_lo"))
    upper = z_hi == 1
    act_fwd, act_rev = (act_fwd[0], act_rev[0])
    t, d = act_fwd.shape

    def choose(a, b):
        return jnp.where(upper, a, b)

    first = choose(act_rev, act_fwd)
    hop = [((y - 1) % Y * 2 + 1, y * 2 + 1) for y in range(Y)]
    hop += [((y + 1) % Y * 2, y * 2) for y in range(Y)]
    second = lax.ppermute(choose(act_fwd, act_rev), ("y", "z_hi"), hop)

    def ring(block):
        full = lax.all_gather(block, ("z_hi", "z_lo"), axis=0, tiled=True)
        return full

    def arrived(full):
        return lax.dynamic_slice_in_dim(full, (1 - z_hi) * Z * t, Z * t, 0)

    def at_home(full):
        return lax.dynamic_slice_in_dim(full, ((1 - z_hi) * Z + z_lo) * t, t, 0)

    full_1 = ring(first)
    ids = [choose(ids_fwd[0], ids_rev[0]), choose(ids_rev[0], ids_fwd[0])]
    probs = [choose(probs_fwd[0], probs_rev[0]), choose(probs_rev[0], probs_fwd[0])]
    slots = [slots_of(i) for i in ids]
    slots_all = lax.all_gather(jnp.stack(slots), "z_lo", axis=0)
    swap = [(0, 1), (1, 0)]
    gate_w = jnp.concatenate([w_gate[0], lax.ppermute(w_gate[0], "core", swap)], axis=1)
    up_w = jnp.concatenate([w_up[0], lax.ppermute(w_up[0], "core", swap)], axis=1)
    down_w = jnp.concatenate([w_down[0], lax.ppermute(w_down[0], "core", swap)], axis=0)
    full_2 = ring(after(second, full_1))
    outs = []
    for p, full in enumerate((full_1, full_2)):
        sent = outgoing(arrived(full), slots_all[:, p], z_lo)
        rows = lax.all_to_all(sent, "x", split_axis=0, concat_axis=0, tiled=True)
        done = expert(rows, gate_w, up_w, down_w)
        back = lax.all_to_all(done, ("x", "z_lo"), split_axis=0, concat_axis=0, tiled=True)
        outs.append(combine(at_home(full), back, slots[p], probs[p]))
    return (choose(outs[0], outs[1])[None], choose(outs[1], outs[0])[None])


def solution(mesh):
    split = Mesh(mesh.devices.reshape(Y, 2, X, Z, 2), ("y", "z_hi", "x", "z_lo", "core"))
    section, spread = (("y", "z_hi"), ("x", "z_lo", "core"))
    tokens = P(section, spread, None)
    return jax.shard_map(
        body,
        mesh=split,
        in_specs=(tokens,) * 6 + (P(section, None, spread),) * 2 + (tokens,),
        out_specs=(tokens, tokens),
        check_vma=False,
    )
```

profile of v0, /device:TPU:1, one launch (start us, length us, event | category | flops | bytes accessed | tf_op | source)
XLA Modules:
  0.0 419.6 jit_solution(7810823616252128842)
XLA Ops:
  7.2 2.7 broadcast_select_fusion
  10.0 3.6 collective-permute-start.3
  13.6 21.8 %collective-permute-done.3 = bf16[128,4096]{1,0:T(8,128)(2,1)S(1)} collective-permute-done((bf16[128,4096]{1,0:T(8,128)(2,1)S(1)}, bf16[128,4096]{1,0:T(8,128)(2,1)S(1)}, u32[]{:S(2)}, u32[]{:S(2)}) %collective-permute-start.3) | collective-permute-done | bytes 1048608 | tf_op jit(solution)/shard_map/ppermute | solution.py:73
  36.4 1.6 collective-permute-start.1
  39.5 11.1 %all-gather.1 = s32[8,128,2]{1,2,0:T(2,128)S(1)} all-gather(s32[2,128,2]{1,2,0:T(2,128)S(1)} %pad_add_fusion), channel_id=3, replica_groups=mesh['y'=4,'z_hi'=2,'x'=4,'z_lo'=4,'core'=2] {'z_lo'}, dimensions={0}, use_global_device_ids=true | all-gather | bytes 10240 | tf_op jit(solution)/shard_map/all_gather | solution.py:89
  50.6 57.7 %all-gather.7.cloned.1.call-done = bf16[1,1024,4096]{2,1,0:T(8,128)(2,1)} async-done(((bf16[1,128,4096]{2,1,0:T(8,128)(2,1)}), bf16[1,1024,4096]{2,1,0:T(8,128)(2,1)}) %all-gather.7.cloned.1.call-update) | async-done | bytes 8388624 | tf_op jit(solution)/shard_map/all_gather | solution.py:76
  108.3 5.7 %convolution_convert_fusion.1 = bf16[384,4096]{1,0:T(8,128)(2,1)} fusion(bf16[1,1024,4096]{2,1,0:T(8,128)(2,1)} %all-gather.7.cloned.1.call-done, s32[]{:T(128)S(6)} %select_n.182, s32[512]{0:T(512)S(1)} %add_select_fusion.2, s32[512]{0:T(512)S(1)} %bitcast.58, s32[512]{0:T(512)S(1)} %bitcast.57, s32[384]{0:T(512)S(1)} %get-tuple-element.29, ...), kind=kOutput, calls=%fused_computation.4 | convolution fusion | flops 1613168640 | bytes 7349252 | tf_op jit(solution)/shard_map/dot_general | solution.py:34
  114.0 4.0 all-to-all-start
  119.0 84.6 %all-gather.5.cloned.1.call-done = bf16[1024,4096]{1,0:T(8,128)(2,1)} async-done(((bf16[128,4096]{1,0:T(8,128)(2,1)}), bf16[1024,4096]{1,0:T(8,128)(2,1)}) %all-gather.5.cloned.1.call-update) | async-done | bytes 8388624 | tf_op jit(solution)/shard_map/all_gather | solution.py:76
  203.6 5.7 %convolution_convert_fusion = bf16[384,4096]{1,0:T(8,128)(2,1)} fusion(bf16[1024,4096]{1,0:T(8,128)(2,1)} %all-gather.5.cloned.1.call-done, s32[]{:T(128)S(6)} %select_n.182, s32[512]{0:T(512)S(1)} %bitcast.56, s32[512]{0:T(512)S(1)} %bitcast.55, s32[512]{0:T(512)S(1)} %add_select_fusion.2, s32[384]{0:T(512)S(1)} %get-tuple-element.29, ...), kind=kOutput, calls=%fused_computation.3 | convolution fusion | flops 1613168640 | bytes 7349252 | tf_op jit(solution)/shard_map/dot_general | solution.py:34
  209.3 4.8 %all-to-all-start.2 = ((bf16[4,96,4096]{2,1,0:T(8,128)(2,1)}), bf16[4,96,4096]{2,1,0:T(8,128)(2,1)}, u32[]{:S(2)}, u32[]{:S(2)}) async-start(bf16[4,96,4096]{2,1,0:T(8,128)(2,1)} %bitcast.52), calls=%async_computation.2 | async-start | bytes 6291456 | tf_op jit(solution)/shard_map/all_to_all | solution.py:98
  214.1 6.5 %fusion.4 = f32[384,768]{1,0:T(8,128)} fusion(bf16[384,4096]{1,0:T(8,128)(2,1)S(1)} %bitcast.49, bf16[4096,384]{1,0:T(8,128)(2,1)} %collective-permute-done.1, bf16[4096,384]{1,0:T(8,128)(2,1)} %bitcast.60), kind=kOutput, calls=%fused_computation.11 | convolution fusion | flops 2428502016 | bytes 10616832 | tf_op jit(solution)/shard_map/dot_general | solution.py:39
  220.6 13.3 %convolution_convert_fusion.3 = bf16[384,4096]{1,0:T(8,128)(2,1)} fusion(bf16[384,4096]{1,0:T(8,128)(2,1)} %collective-permute-done.2, bf16[384,4096]{1,0:T(8,128)(2,1)} %bitcast.63, f32[384,768]{1,0:T(8,128)} %fusion.4, bf16[384,4096]{1,0:T(8,128)(2,1)S(1)} %bitcast.50, bf16[4096,384]{1,0:T(8,128)(2,1)} %collective-permute-done, bf16[4096,384]{1,0:T(8,128)(2,1)} %bitcast.66), kind=kOutput, calls=%fused_computation.6 | convolution fusion | flops 4860346368 | bytes 20054016 | tf_op jit(solution)/shard_map/dot_general | solution.py:41
  233.9 17.0 %all-to-all-done.2 = bf16[4,96,4096]{2,1,0:T(8,128)(2,1)} async-done(((bf16[4,96,4096]{2,1,0:T(8,128)(2,1)}), bf16[4,96,4096]{2,1,0:T(8,128)(2,1)}, u32[]{:S(2)}, u32[]{:S(2)}) %all-to-all-start.2) | async-done | bytes 3145760 | tf_op jit(solution)/shard_map/all_to_all | solution.py:98
  250.9 4.7 %all-to-all-start.1 = ((bf16[16,24,4096]{2,1,0:T(8,128)(2,1)}), bf16[16,24,4096]{2,1,0:T(8,128)(2,1)S(1)}, u32[]{:S(2)}, u32[]{:S(2)}) async-start(bf16[16,24,4096]{2,1,0:T(8,128)(2,1)} %bitcast.53), calls=%async_computation.1 | async-start | bytes 6291456 | tf_op jit(solution)/shard_map/all_to_all | solution.py:100
  255.6 7.4 %fusion.3 = f32[384,768]{1,0:T(8,128)} fusion(bf16[384,4096]{1,0:T(8,128)(2,1)} %bitcast.20, bf16[4096,384]{1,0:T(8,128)(2,1)} %collective-permute-done.1, bf16[4096,384]{1,0:T(8,128)(2,1)} %bitcast.61), kind=kOutput, calls=%fused_computation.10 | convolution fusion | flops 2428502016 | bytes 10616832 | tf_op jit(solution)/shard_map/dot_general | solution.py:39
  263.0 14.2 %convolution_convert_fusion.2 = bf16[384,4096]{1,0:T(8,128)(2,1)} fusion(bf16[384,4096]{1,0:T(8,128)(2,1)} %collective-permute-done.2, bf16[384,4096]{1,0:T(8,128)(2,1)} %bitcast.64, f32[384,768]{1,0:T(8,128)} %fusion.3, bf16[384,4096]{1,0:T(8,128)(2,1)} %bitcast.20, bf16[4096,384]{1,0:T(8,128)(2,1)} %collective-permute-done, bf16[4096,384]{1,0:T(8,128)(2,1)} %bitcast.67), kind=kOutput, calls=%fused_computation.5 | convolution fusion | flops 4860346368 | bytes 20054016 | tf_op jit(solution)/shard_map/dot_general | solution.py:41
  277.2 50.7 %all-to-all-done.1 = bf16[16,24,4096]{2,1,0:T(8,128)(2,1)S(1)} async-done(((bf16[16,24,4096]{2,1,0:T(8,128)(2,1)}), bf16[16,24,4096]{2,1,0:T(8,128)(2,1)S(1)}, u32[]{:S(2)}, u32[]{:S(2)}) %all-to-all-start.1) | async-done | bytes 3145760 | tf_op jit(solution)/shard_map/all_to_all | solution.py:100
  327.9 4.6 %all-to-all-start.3 = ((bf16[16,24,4096]{2,1,0:T(8,128)(2,1)}), bf16[16,24,4096]{2,1,0:T(8,128)(2,1)}, u32[]{:S(2)}, u32[]{:S(2)}) async-start(bf16[16,24,4096]{2,1,0:T(8,128)(2,1)} %bitcast.48), calls=%async_computation.3 | async-start | bytes 6291456 | tf_op jit(solution)/shard_map/all_to_all | solution.py:100
  336.3 3.2 fusion.33
  339.5 65.2 %all-to-all-done.3 = bf16[16,24,4096]{2,1,0:T(8,128)(2,1)} async-done(((bf16[16,24,4096]{2,1,0:T(8,128)(2,1)}), bf16[16,24,4096]{2,1,0:T(8,128)(2,1)}, u32[]{:S(2)}, u32[]{:S(2)}) %all-to-all-start.3) | async-done | bytes 3145760 | tf_op jit(solution)/shard_map/all_to_all | solution.py:100
  404.8 3.3 fusion.37
  408.1 3.6 select_bitcast_fusion
  411.7 1.1 select_bitcast_fusion.1
  (57 shorter events, 7.2 us)
Async XLA Ops:
  7.2 101.2 %all-gather.7.cloned.1.call-start = ((), (), s32[]{:S(2)}) async-start(), calls=%async_computation.5 | async-start | bytes 9437184 | tf_op jit(solution)/shard_map/all_gather | solution.py:76
  7.2 30.9 %copy-start.2 = (s32[1,128,2]{1,2,0:T(2,128)S(1)}, s32[1,128,2]{1,2,0:T(2,128)}, u32[]{:S(2)}) copy-start(s32[1,128,2]{1,2,0:T(2,128)} %param.11) | copy-start | bytes 3076
  7.2 31.0 %copy-start.3 = (s32[1,128,2]{1,2,0:T(2,128)S(1)}, s32[1,128,2]{1,2,0:T(2,128)}, u32[]{:S(2)}) copy-start(s32[1,128,2]{1,2,0:T(2,128)} %param.12) | copy-start | bytes 3076
  9.9 193.7 %all-gather.5.cloned.1.call-start = ((), (), s32[]{:S(2)}) async-start(), calls=%async_computation.4 | async-start | bytes 9437184 | tf_op jit(solution)/shard_map/all_gather | solution.py:76
  10.0 25.5 %collective-permute-start.3 = (bf16[128,4096]{1,0:T(8,128)(2,1)S(1)}, bf16[128,4096]{1,0:T(8,128)(2,1)S(1)}, u32[]{:S(2)}, u32[]{:S(2)}) collective-permute-start(bf16[128,4096]{1,0:T(8,128)(2,1)S(1)} %get-tuple-element.10), channel_id=1, source_target_pairs={{224,32},{32,96},{96,160},{160,224},{64,0},{128,64},{192,128},{0,1... | collective-permute-start | bytes 3145736 | tf_op jit(solution)/shard_map/ppermute | solution.py:73
  35.4 1.0 copy-start.1
  36.4 177.7 %collective-permute-start.1 = (bf16[4096,384]{1,0:T(8,128)(2,1)}, bf16[4096,384]{1,0:T(8,128)(2,1)}, u32[]{:S(2)}, u32[]{:S(2)}) collective-permute-start(bf16[4096,384]{1,0:T(8,128)(2,1)} %bitcast.59), channel_id=1, source_target_pairs={{0,1},{1,0},{2,3},{3,2},{4,5},{5,4},{6,7},{7,6},{8,9},{9,8},{10,11... | collective-permute-start | bytes 9437192 | tf_op jit(solution)/shard_map/ppermute | solution.py:92
  114.0 95.2 %all-to-all-start = ((bf16[4,96,4096]{2,1,0:T(8,128)(2,1)}), bf16[4,96,4096]{2,1,0:T(8,128)(2,1)S(1)}, u32[]{:S(2)}, u32[]{:S(2)}) async-start(bf16[4,96,4096]{2,1,0:T(8,128)(2,1)} %bitcast.51), calls=%async_computation | async-start | bytes 6291456 | tf_op jit(solution)/shard_map/all_to_all | solution.py:98
  118.0 102.6 %collective-permute-start = (bf16[4096,384]{1,0:T(8,128)(2,1)}, bf16[4096,384]{1,0:T(8,128)(2,1)}, u32[]{:S(2)}, u32[]{:S(2)}) collective-permute-start(bf16[4096,384]{1,0:T(8,128)(2,1)} %bitcast.65), channel_id=1, source_target_pairs={{0,1},{1,0},{2,3},{3,2},{4,5},{5,4},{6,7},{7,6},{8,9},{9,8},{10,11... | collective-permute-start | bytes 9437192 | tf_op jit(solution)/shard_map/ppermute | solution.py:91
  119.0 101.6 %collective-permute-start.2 = (bf16[384,4096]{1,0:T(8,128)(2,1)}, bf16[384,4096]{1,0:T(8,128)(2,1)}, u32[]{:S(2)}, u32[]{:S(2)}) collective-permute-start(bf16[384,4096]{1,0:T(8,128)(2,1)} %bitcast.62), channel_id=1, source_target_pairs={{0,1},{1,0},{2,3},{3,2},{4,5},{5,4},{6,7},{7,6},{8,9},{9,8},{10,11... | collective-permute-start | bytes 9437192 | tf_op jit(solution)/shard_map/ppermute | solution.py:93
  209.3 41.7 %all-to-all-start.2 = ((bf16[4,96,4096]{2,1,0:T(8,128)(2,1)}), bf16[4,96,4096]{2,1,0:T(8,128)(2,1)}, u32[]{:S(2)}, u32[]{:S(2)}) async-start(bf16[4,96,4096]{2,1,0:T(8,128)(2,1)} %bitcast.52), calls=%async_computation.2 | async-start | bytes 6291456 | tf_op jit(solution)/shard_map/all_to_all | solution.py:98
  250.9 77.0 %all-to-all-start.1 = ((bf16[16,24,4096]{2,1,0:T(8,128)(2,1)}), bf16[16,24,4096]{2,1,0:T(8,128)(2,1)S(1)}, u32[]{:S(2)}, u32[]{:S(2)}) async-start(bf16[16,24,4096]{2,1,0:T(8,128)(2,1)} %bitcast.53), calls=%async_computation.1 | async-start | bytes 6291456 | tf_op jit(solution)/shard_map/all_to_all | solution.py:100
  327.9 4.9 %copy-start.4 = (f32[1,128,2]{1,2,0:T(2,128)S(1)}, f32[1,128,2]{1,2,0:T(2,128)}, u32[]{:S(2)}) copy-start(f32[1,128,2]{1,2,0:T(2,128)} %param.13) | copy-start | bytes 3076
  327.9 5.0 %copy-start.5 = (f32[1,128,2]{1,2,0:T(2,128)S(1)}, f32[1,128,2]{1,2,0:T(2,128)}, u32[]{:S(2)}) copy-start(f32[1,128,2]{1,2,0:T(2,128)} %param.14) | copy-start | bytes 3076
  327.9 76.9 %all-to-all-start.3 = ((bf16[16,24,4096]{2,1,0:T(8,128)(2,1)}), bf16[16,24,4096]{2,1,0:T(8,128)(2,1)}, u32[]{:S(2)}, u32[]{:S(2)}) async-start(bf16[16,24,4096]{2,1,0:T(8,128)(2,1)} %bitcast.48), calls=%async_computation.3 | async-start | bytes 6291456 | tf_op jit(solution)/shard_map/all_to_all | solution.py:100
  404.8 3.3 copy-start
Sparse Core Ops, SparseCore 0:
  10.4 97.9 all-gather.6
  110.7 92.8 all-gather.4
where the time goes:
time: 420 us
  waiting for transfers between devices  297 us (71%)
  matrix products  59.7 us (14%)
  starting transfers between devices  24.4 us (6%)
  between operations  14.3 us (3%)
  blocking collectives  11.1 us (3%)
  other arithmetic  8.69 us (2%)
  local copies, waits for them, and re-layouts  4.35 us (1%)
    all_gather x2, waiting for transfers between devices, ring(): full = lax.all_gather(block, ('z_hi', 'z_lo'), axis=0, tiled=True)  142 us
    all_to_all x2, waiting for transfers between devices, body(): lax.all_to_all(done, ('x', 'z_lo'), split_axis=0, concat_axis=0, tiled=True)  116 us
    dot_general x2, matrix products, expert(): return jnp.dot(hidden, w_down, preferred_element_type=F32).astype(BF)  27.5 us
    ppermute x1, waiting for transfers between devices, body(): second = lax.ppermute(choose(act_fwd, act_rev), ('y', 'z_hi'), hop)  21.8 us
    all_to_all x2, waiting for transfers between devices, body(): rows = lax.all_to_all(sent, 'x', split_axis=0, concat_axis=0, tiled=True)  17 us
    dot_general x2, matrix products, expert(): up = jnp.dot(rows, w_up, preferred_element_type=F32)  13.8 us
    dot_general x2, matrix products, outgoing(): return jnp.dot(pick, tokens, preferred_element_type=F32).astype(BF)  11.4 us
    all_gather x1, blocking collectives, body(): slots_all = lax.all_gather(jnp.stack(slots), 'z_lo', axis=0)  11.1 us
  transfers between devices with their start and end apart: 10, of which 6 were waited for; matrix products, arithmetic and copies ran while one was open for 15% of the time, Pallas kernels for 0%

commit v1 on v0

--- a/solution.py
+++ b/solution.py
@@ -73,7 +73,12 @@
     second = lax.ppermute(choose(act_fwd, act_rev), ("y", "z_hi"), hop)
 
     def ring(block):
-        full = lax.all_gather(block, ("z_hi", "z_lo"), axis=0, tiled=True)
+        full = jnp.concatenate(
+            lax.all_to_all(
+                jnp.stack([block] * lax.axis_size(("z_hi", "z_lo"))), ("z_hi", "z_lo"), 0, 0
+            ),
+            axis=0,
+        )
         return full
 
     def arrived(full):

time: 420 us -> 646 us (1.54)
  blocking collectives: 11.1 us -> 185 us
  waiting for transfers between devices: 297 us -> 342 us
  starting transfers between devices: 24.4 us -> 38 us
  between operations: 14.3 us -> 0.87 us
  local copies, waits for them, and re-layouts: 4.35 us -> 12 us
    all_gather x1, blocking collectives: 11.1 us -> 185 us  [body(): slots_all = lax.all_gather(jnp.stack(slots), 'z_lo', axis=0)]
    all_to_all x0 -> x2, waiting for transfers between devices: none -> 163 us  [ring(): lax.all_to_all(jnp.stack([block] * lax.axis_size(('z_hi', 'z_lo'))), ('z_...]
    all_gather x2 -> x0, waiting for transfers between devices: 142 us -> none  [ring(): full = lax.all_gather(block, ('z_hi', 'z_lo'), axis=0, tiled=True)]
    all_to_all x2, waiting for transfers between devices: 17 us -> 41.9 us  [body(): rows = lax.all_to_all(sent, 'x', split_axis=0, concat_axis=0, tiled=True)]
    all_to_all x0 -> x2, starting transfers between devices: none -> 14.2 us  [ring(): lax.all_to_all(jnp.stack([block] * lax.axis_size(('z_hi', 'z_lo'))), ('z_...]
    another operation x0 -> x2, local copies, waits for them, and re-layouts: none -> 8.65 us  [ring(): jnp.stack([block] * lax.axis_size(('z_hi', 'z_lo')))]
  transfers between devices with their start and end apart: 10 -> 10, of which waited for: 6 -> 6; matrix products, arithmetic and copies ran while one was open for 15% -> 10% of each run, Pallas kernels for 0% -> 0%
where the time goes in v1:
time: 646 us; the launch traced here: 645 us
  waiting for transfers between devices  342 us (53%)
  blocking collectives  185 us (29%)
  matrix products  60 us (9%)
  starting transfers between devices  38 us (6%)
  local copies, waits for them, and re-layouts  12 us (2%)
  other arithmetic  7.71 us (1%)
    all_gather x1, blocking collectives, body(): slots_all = lax.all_gather(jnp.stack(slots), 'z_lo', axis=0)  185 us
    all_to_all x2, waiting for transfers between devices, ring(): lax.all_to_all(jnp.stack([block] * lax.axis_size(('z_hi', 'z_lo'))), ('z_...  163 us
    all_to_all x2, waiting for transfers between devices, body(): lax.all_to_all(done, ('x', 'z_lo'), split_axis=0, concat_axis=0, tiled=True)  116 us
    all_to_all x2, waiting for transfers between devices, body(): rows = lax.all_to_all(sent, 'x', split_axis=0, concat_axis=0, tiled=True)  41.9 us
    dot_general x2, matrix products, expert(): return jnp.dot(hidden, w_down, preferred_element_type=F32).astype(BF)  27.6 us
    ppermute x1, waiting for transfers between devices, body(): second = lax.ppermute(choose(act_fwd, act_rev), ('y', 'z_hi'), hop)  21.5 us
    all_to_all x2, starting transfers between devices, ring(): lax.all_to_all(jnp.stack([block] * lax.axis_size(('z_hi', 'z_lo'))), ('z_...  14.2 us
    dot_general x2, matrix products, expert(): up = jnp.dot(rows, w_up, preferred_element_type=F32)  13.8 us
  transfers between devices with their start and end apart: 10, of which 6 were waited for; matrix products, arithmetic and copies ran while one was open for 10% of the time, Pallas kernels for 0%

profile of v1, /device:TPU:1, one launch (start us, length us, event | category | flops | bytes accessed | tf_op | source)
XLA Modules:
  0.0 645.2 jit_solution(140534693768900510)
XLA Ops:
  2.3 4.3 stack.9
  6.6 9.0 %all-to-all-start = ((bf16[8,128,4096]{2,1,0:T(8,128)(2,1)}), bf16[8,128,4096]{2,1,0:T(8,128)(2,1)}, u32[]{:S(2)}, u32[]{:S(2)}) async-start(bf16[8,128,4096]{2,1,0:T(8,128)(2,1)} %stack.9), calls=%async_computation | async-start | bytes 16777216 | tf_op jit(solution)/shard_map/all_to_all | solution.py:77
  18.4 21.5 %collective-permute-done.3 = bf16[128,4096]{1,0:T(8,128)(2,1)S(1)} collective-permute-done((bf16[128,4096]{1,0:T(8,128)(2,1)S(1)}, bf16[128,4096]{1,0:T(8,128)(2,1)S(1)}, u32[]{:S(2)}, u32[]{:S(2)}) %collective-permute-start.3) | collective-permute-done | bytes 1048608 | tf_op jit(solution)/shard_map/ppermute | solution.py:73
  39.9 162.8 %all-to-all-done = bf16[8,128,4096]{2,1,0:T(8,128)(2,1)} async-done(((bf16[8,128,4096]{2,1,0:T(8,128)(2,1)}), bf16[8,128,4096]{2,1,0:T(8,128)(2,1)}, u32[]{:S(2)}, u32[]{:S(2)}) %all-to-all-start) | async-done | bytes 8388640 | tf_op jit(solution)/shard_map/all_to_all | solution.py:77
  202.7 4.4 stack.11
  207.1 5.2 all-to-all-start.3
  214.2 184.6 %all-gather = s32[8,128,2]{1,2,0:T(2,128)S(1)} all-gather(s32[2,128,2]{1,2,0:T(2,128)S(1)} %pad_add_fusion), channel_id=2, replica_groups=mesh['y'=4,'z_hi'=2,'x'=4,'z_lo'=4,'core'=2] {'z_lo'}, dimensions={0}, use_global_device_ids=true | all-gather | bytes 10240 | tf_op jit(solution)/shard_map/all_gather | solution.py:94
  398.9 5.8 convolution_convert_fusion.1
  404.7 4.0 all-to-all-start.1
  410.9 5.8 convolution_convert_fusion
  416.7 27.3 %all-to-all-done.1 = bf16[4,96,4096]{2,1,0:T(8,128)(2,1)S(1)} async-done(((bf16[4,96,4096]{2,1,0:T(8,128)(2,1)}), bf16[4,96,4096]{2,1,0:T(8,128)(2,1)S(1)}, u32[]{:S(2)}, u32[]{:S(2)}) %all-to-all-start.1) | async-done | bytes 3145760 | tf_op jit(solution)/shard_map/all_to_all | solution.py:103
  444.1 4.8 all-to-all-start.4
  448.9 6.5 %fusion.3 = f32[384,768]{1,0:T(8,128)} fusion(bf16[384,4096]{1,0:T(8,128)(2,1)S(1)} %bitcast.46, bf16[4096,384]{1,0:T(8,128)(2,1)} %collective-permute-done.1, bf16[4096,384]{1,0:T(8,128)(2,1)} %bitcast.10), kind=kOutput, calls=%fused_computation.10 | convolution fusion | flops 2428502016 | bytes 10616832 | tf_op jit(solution)/shard_map/dot_general | solution.py:39
  455.4 13.3 %convolution_convert_fusion.3 = bf16[384,4096]{1,0:T(8,128)(2,1)} fusion(bf16[384,4096]{1,0:T(8,128)(2,1)} %collective-permute-done.2, bf16[384,4096]{1,0:T(8,128)(2,1)} %bitcast.57, f32[384,768]{1,0:T(8,128)} %fusion.3, bf16[384,4096]{1,0:T(8,128)(2,1)S(1)} %bitcast.47, bf16[4096,384]{1,0:T(8,128)(2,1)} %collective-permute-done, bf16[4096,384]{1,0:T(8,128)(2,1)} %bitcast.60), kind=kOutput, calls=%fused_computation.6 | convolution fusion | flops 4860346368 | bytes 20054016 | tf_op jit(solution)/shard_map/dot_general | solution.py:41
  468.7 14.5 %all-to-all-done.4 = bf16[4,96,4096]{2,1,0:T(8,128)(2,1)} async-done(((bf16[4,96,4096]{2,1,0:T(8,128)(2,1)}), bf16[4,96,4096]{2,1,0:T(8,128)(2,1)}, u32[]{:S(2)}, u32[]{:S(2)}) %all-to-all-start.4) | async-done | bytes 3145760 | tf_op jit(solution)/shard_map/all_to_all | solution.py:103
  483.2 4.7 all-to-all-start.2
  488.0 7.4 %fusion.2 = f32[384,768]{1,0:T(8,128)} fusion(bf16[384,4096]{1,0:T(8,128)(2,1)} %bitcast.21, bf16[4096,384]{1,0:T(8,128)(2,1)} %collective-permute-done.1, bf16[4096,384]{1,0:T(8,128)(2,1)} %bitcast.10), kind=kOutput, calls=%fused_computation.9 | convolution fusion | flops 2428502016 | bytes 10616832 | tf_op jit(solution)/shard_map/dot_general | solution.py:39
  495.4 14.3 %convolution_convert_fusion.2 = bf16[384,4096]{1,0:T(8,128)(2,1)} fusion(bf16[384,4096]{1,0:T(8,128)(2,1)} %collective-permute-done.2, bf16[384,4096]{1,0:T(8,128)(2,1)} %bitcast.58, f32[384,768]{1,0:T(8,128)} %fusion.2, bf16[384,4096]{1,0:T(8,128)(2,1)} %bitcast.21, bf16[4096,384]{1,0:T(8,128)(2,1)} %collective-permute-done, bf16[4096,384]{1,0:T(8,128)(2,1)} %bitcast.61), kind=kOutput, calls=%fused_computation.5 | convolution fusion | flops 4860346368 | bytes 20054016 | tf_op jit(solution)/shard_map/dot_general | solution.py:41
  509.7 50.5 %all-to-all-done.2 = bf16[16,24,4096]{2,1,0:T(8,128)(2,1)S(1)} async-done(((bf16[16,24,4096]{2,1,0:T(8,128)(2,1)}), bf16[16,24,4096]{2,1,0:T(8,128)(2,1)S(1)}, u32[]{:S(2)}, u32[]{:S(2)}) %all-to-all-start.2) | async-done | bytes 3145760 | tf_op jit(solution)/shard_map/all_to_all | solution.py:105
  560.2 4.6 all-to-all-start.5
  568.7 3.2 fusion.32
  571.9 65.3 %all-to-all-done.5 = bf16[16,24,4096]{2,1,0:T(8,128)(2,1)} async-done(((bf16[16,24,4096]{2,1,0:T(8,128)(2,1)}), bf16[16,24,4096]{2,1,0:T(8,128)(2,1)}, u32[]{:S(2)}, u32[]{:S(2)}) %all-to-all-start.5) | async-done | bytes 3145760 | tf_op jit(solution)/shard_map/all_to_all | solution.py:105
  637.2 3.3 fusion.36
  640.5 3.6 select_bitcast_fusion
  (55 shorter events, 13.4 us)
Async XLA Ops:
  6.6 196.1 %all-to-all-start = ((bf16[8,128,4096]{2,1,0:T(8,128)(2,1)}), bf16[8,128,4096]{2,1,0:T(8,128)(2,1)}, u32[]{:S(2)}, u32[]{:S(2)}) async-start(bf16[8,128,4096]{2,1,0:T(8,128)(2,1)} %stack.9), calls=%async_computation | async-start | bytes 16777216 | tf_op jit(solution)/shard_map/all_to_all | solution.py:77
  15.6 24.2 %collective-permute-start.3 = (bf16[128,4096]{1,0:T(8,128)(2,1)S(1)}, bf16[128,4096]{1,0:T(8,128)(2,1)S(1)}, u32[]{:S(2)}, u32[]{:S(2)}) collective-permute-start(bf16[128,4096]{1,0:T(8,128)(2,1)S(1)} %get-tuple-element.10), channel_id=1, source_target_pairs={{224,32},{32,96},{96,160},{160,224},{64,0},{128,64},{192,128},{0,1... | collective-permute-start | bytes 3145736 | tf_op jit(solution)/shard_map/ppermute | solution.py:73
  207.1 5.8 copy-start.1
  207.1 5.9 copy-start.2
  207.1 197.6 %all-to-all-start.3 = ((bf16[8,128,4096]{2,1,0:T(8,128)(2,1)}), bf16[8,128,4096]{2,1,0:T(8,128)(2,1)}, u32[]{:S(2)}, u32[]{:S(2)}) async-start(bf16[8,128,4096]{2,1,0:T(8,128)(2,1)} %stack.11), calls=%async_computation.3 | async-start | bytes 16777216 | tf_op jit(solution)/shard_map/all_to_all | solution.py:77
  212.2 236.7 %collective-permute-start.1 = (bf16[4096,384]{1,0:T(8,128)(2,1)}, bf16[4096,384]{1,0:T(8,128)(2,1)}, u32[]{:S(2)}, u32[]{:S(2)}) collective-permute-start(bf16[4096,384]{1,0:T(8,128)(2,1)} %bitcast.10), channel_id=1, source_target_pairs={{0,1},{1,0},{2,3},{3,2},{4,5},{5,4},{6,7},{7,6},{8,9},{9,8},{10,11... | collective-permute-start | bytes 9437192 | tf_op jit(solution)/shard_map/ppermute | solution.py:97
  404.7 39.4 %all-to-all-start.1 = ((bf16[4,96,4096]{2,1,0:T(8,128)(2,1)}), bf16[4,96,4096]{2,1,0:T(8,128)(2,1)S(1)}, u32[]{:S(2)}, u32[]{:S(2)}) async-start(bf16[4,96,4096]{2,1,0:T(8,128)(2,1)} %bitcast.48), calls=%async_computation.1 | async-start | bytes 6291456 | tf_op jit(solution)/shard_map/all_to_all | solution.py:103
  408.7 46.7 %collective-permute-start.2 = (bf16[384,4096]{1,0:T(8,128)(2,1)}, bf16[384,4096]{1,0:T(8,128)(2,1)}, u32[]{:S(2)}, u32[]{:S(2)}) collective-permute-start(bf16[384,4096]{1,0:T(8,128)(2,1)} %bitcast.56), channel_id=1, source_target_pairs={{0,1},{1,0},{2,3},{3,2},{4,5},{5,4},{6,7},{7,6},{8,9},{9,8},{10,11... | collective-permute-start | bytes 9437192 | tf_op jit(solution)/shard_map/ppermute | solution.py:98
  410.9 44.5 %collective-permute-start = (bf16[4096,384]{1,0:T(8,128)(2,1)}, bf16[4096,384]{1,0:T(8,128)(2,1)}, u32[]{:S(2)}, u32[]{:S(2)}) collective-permute-start(bf16[4096,384]{1,0:T(8,128)(2,1)} %bitcast.59), channel_id=1, source_target_pairs={{0,1},{1,0},{2,3},{3,2},{4,5},{5,4},{6,7},{7,6},{8,9},{9,8},{10,11... | collective-permute-start | bytes 9437192 | tf_op jit(solution)/shard_map/ppermute | solution.py:96
  444.1 39.2 %all-to-all-start.4 = ((bf16[4,96,4096]{2,1,0:T(8,128)(2,1)}), bf16[4,96,4096]{2,1,0:T(8,128)(2,1)}, u32[]{:S(2)}, u32[]{:S(2)}) async-start(bf16[4,96,4096]{2,1,0:T(8,128)(2,1)} %bitcast.49), calls=%async_computation.4 | async-start | bytes 6291456 | tf_op jit(solution)/shard_map/all_to_all | solution.py:103
  483.2 77.0 %all-to-all-start.2 = ((bf16[16,24,4096]{2,1,0:T(8,128)(2,1)}), bf16[16,24,4096]{2,1,0:T(8,128)(2,1)S(1)}, u32[]{:S(2)}, u32[]{:S(2)}) async-start(bf16[16,24,4096]{2,1,0:T(8,128)(2,1)} %bitcast.50), calls=%async_computation.2 | async-start | bytes 6291456 | tf_op jit(solution)/shard_map/all_to_all | solution.py:105
  560.2 5.0 copy-start.3
  560.2 5.1 copy-start.4
  560.2 77.0 %all-to-all-start.5 = ((bf16[16,24,4096]{2,1,0:T(8,128)(2,1)}), bf16[16,24,4096]{2,1,0:T(8,128)(2,1)}, u32[]{:S(2)}, u32[]{:S(2)}) async-start(bf16[16,24,4096]{2,1,0:T(8,128)(2,1)} %bitcast.45), calls=%async_computation.5 | async-start | bytes 6291456 | tf_op jit(solution)/shard_map/all_to_all | solution.py:105
  637.2 3.3 copy-start
